TPU v7x, 32 devices: a whole 2x2x4 slice. The times are simulated.
32 devices in a mesh: space: 16 (over z, y, core), chan: 2 (over x).
Axes of the slice: x: 2, y: 2, z: 4, core: 2. Of those that a mesh axis runs over, the one named last changes fastest.
Arguments:
- features: bfloat16 [1, 128, 32, 2048], P(None, 'chan', 'space'), may hold values from -6 to 6
- top_map: int32 [16, 2048], P('space'), may hold values from 0 to 2048, as said below
- bottom_map: int32 [16, 2048], P('space'), may hold values from 0 to 2048, as said below
- first_weight: bfloat16 [128, 3, 3, 128], P('chan'), may hold values from -0.1875 to 0.1875
- first_bias: float32 [128], P('chan'), may hold values from -3 to 3
- second_weight: bfloat16 [256, 3, 3, 128], P('chan'), may hold values from -0.1875 to 0.1875
- second_bias: float32 [256], P('chan'), may hold values from -3 to 3
Outputs:
- hidden: bfloat16 [1, 128, 32, 2048], P(None, 'chan', 'space')
- coarse: bfloat16 [1, 256, 16, 1024], P(None, 'chan', 'space')
Inputs may be any that keep to these rules, and one draw needn't show every extreme that they name: `top_map`: each entry of row s, column k is k - 1, k or k + 1 taken modulo 2048, or 2048 for a missing neighbour at a face corner; exactly 4 entries of each row equal 2048. `bottom_map`: each entry of row s, column k is k - 1, k or k + 1 taken modulo 2048, or 2048 for a missing neighbour at a face corner; exactly 4 entries of each row equal 2048.
All inputs are finite; a program needn't handle non-finite values.
Results may differ from a plain program's by a relative error of at most 0.012.
Values may be sent and summed in bfloat16 or wider, within the bound.
A program may use at most 64 MiB of HBM per device.

v0:
```python
import functools

import jax
import jax.numpy as jnp
from jax import lax
from jax.experimental import pallas as pl
from jax.experimental.pallas import tpu as pltpu
from jax.sharding import PartitionSpec as P

MESH = pl.DeviceIdType.MESH
BF16 = jnp.bfloat16
F32 = jnp.float32
EDGE = 128
SPREAD = 256
PIECES = 4


def gelu(v):
    return 0.5 * v * (1.0 + jnp.tanh(0.7978845608028654 * (v + 0.044715 * (v * v * v))))


def remap(raw, pick):
    value = raw.astype(F32)
    found = jnp.where(pick == 1, value, 0.0)
    found = jnp.where(pick == 2, pltpu.roll(value, 1, 1), found)
    found = jnp.where(pick == 3, pltpu.roll(value, value.shape[1] - 1, 1), found)
    return found.astype(BF16)


def as_column(row):
    count = row.shape[1]
    down = lax.broadcasted_iota(jnp.int32, (count, count), 0)
    across = lax.broadcasted_iota(jnp.int32, (count, count), 1)
    return jnp.sum(jnp.where(down == across, jnp.broadcast_to(row, (count, count)), 0.0), axis=1, keepdims=True)


def kernel(
    space, chan, x_ref, top_ref, bottom_ref, w1_ref, b1_ref, w2_ref, b2_ref, hidden_ref, coarse_ref,
    padded, upper, lower, wide1, wide2, b1_all, b2_all, totals, hid, rim, even, odd, sums, result,
    x_send, x_recv, up_send, up_recv, low_send, low_recv, rim_send, rim_recv,
    own_sem, w_send, w_recv, f_send, f_recv, b_send, b_recv, h_send, h_recv, p_send, p_recv,
):
    s = lax.axis_index("space")
    j = lax.axis_index("chan")
    _, c, width = x_ref.shape
    channels = chan * c
    o = w1_ref.shape[2]
    o2 = w2_ref.shape[2]
    part = width // chan
    window = part + 2 * EDGE
    half = part // 2
    has_above = s > 0
    has_below = s < space - 1
    core = lax.rem(s, 2)
    mate = s + 1 - 2 * core

    def peer(k):
        return lax.rem(j + k, chan)

    def source(k):
        return lax.rem(j + chan - k, chan)

    def remote(src, dst, send, recv, where):
        return pltpu.make_async_remote_copy(
            src_ref=src, dst_ref=dst, send_sem=send, recv_sem=recv, device_id=where, device_id_type=MESH
        )

    barrier = pltpu.get_barrier_semaphore()
    for k in range(1, chan):
        pl.semaphore_signal(barrier, inc=1, device_id=(s, peer(k)), device_id_type=MESH)

    @pl.when(has_above)
    def _():
        pl.semaphore_signal(barrier, inc=1, device_id=(s - 1, j), device_id_type=MESH)

    @pl.when(has_below)
    def _():
        pl.semaphore_signal(barrier, inc=1, device_id=(s + 1, j), device_id_type=MESH)

    spans = ((0, EDGE), (EDGE, half), (EDGE + half, half), (EDGE + part, EDGE))

    def there(q):
        return pl.ds(spans[q][0], spans[q][1])

    def across(owner, q):
        begin = lax.rem(owner * part + width - EDGE + spans[q][0], width)
        return pl.ds(pl.multiple_of(begin, EDGE), spans[q][1])

    def x_copy(k, q):
        return remote(
            x_ref.at[:, :, across(peer(k), q)], padded.at[1:3, j, :, there(q)],
            x_send.at[k, q], x_recv.at[k, q], (s, peer(k)),
        )

    def up_copy(k, q):
        src = x_ref.at[1, :, across(j, q)] if k == 0 else padded.at[2, source(k), :, there(q)]
        return remote(src, upper.at[source(k), :, there(q)], up_send.at[k, q], up_recv.at[k, q], (s + 1, j))

    def low_copy(k, q):
        src = x_ref.at[0, :, across(j, q)] if k == 0 else padded.at[1, source(k), :, there(q)]
        return remote(src, lower.at[source(k), :, there(q)], low_send.at[k, q], low_recv.at[k, q], (s - 1, j))

    def pass_on(k, q):
        @pl.when(has_below)
        def _():
            up_copy(k, q).start()

        @pl.when(has_above)
        def _():
            low_copy(k, q).start()

    def place(which, owner, a):
        wide = (wide1, wide2)[which]
        return wide.at[:, owner, :, a * channels : (a + 1) * channels]

    def w_own(which, a):
        return pltpu.make_async_copy((w1_ref, w2_ref)[which].at[a], place(which, j, a), own_sem.at[which, a])

    def w_copy(which, a, k):
        return remote(
            (w1_ref, w2_ref)[which].at[a], place(which, j, a),
            w_send.at[which, a, k], w_recv.at[which, a, k], (s, peer(k)),
        )

    def w_pass(which, a, k):
        return remote(
            place(which, source(k), a), place(which, source(k), a),
            f_send.at[which, a, k], f_recv.at[which, a, k], (mate, j),
        )

    shares = (((0, 0), (0, 1), (1, 0)), ((0, 2), (1, 1), (1, 2)))

    def each_weight(which, mine, others):
        for side in range(2):
            @pl.when(core == side)
            def _():
                for w, a in shares[side]:
                    if w == which:
                        for k in range(1, chan):
                            mine(w, a, k)
                for w, a in shares[1 - side]:
                    if w == which:
                        for k in range(1, chan):
                            others(w, a, k)

    def nothing(w, a, k):
        pass

    def b_copy(which, k):
        ref = (b1_ref, b2_ref)[which]
        dst = (b1_all, b2_all)[which]
        return remote(ref, dst.at[j], b_send.at[which, k], b_recv.at[which, k], (s, peer(k)))

    for which in range(2):
        for a in range(3):
            w_own(which, a).start()
    pl.semaphore_wait(barrier, chan - 1 + jnp.where(has_above, 1, 0) + jnp.where(has_below, 1, 0))
    for q in range(PIECES):
        for k in range(1, chan):
            x_copy(k, q).start()
    for q in range(PIECES):
        pass_on(0, q)
    for k in range(1, chan):
        b_copy(0, k).start()
        b_copy(1, k).start()
    each_weight(0, lambda w, a, k: w_copy(w, a, k).start(), nothing)
    each_weight(1, lambda w, a, k: w_copy(w, a, k).start(), nothing)

    for q in range(PIECES):
        padded[1:3, j, :, there(q)] = x_ref[:, :, across(j, q)]
    b1_all[j] = b1_ref[...]
    b2_all[j] = b2_ref[...]

    @pl.when(s == 0)
    def _():
        upper[...] = jnp.zeros_like(upper)
        rim[...] = jnp.zeros_like(rim)

    @pl.when(s == space - 1)
    def _():
        lower[...] = jnp.zeros_like(lower)

    column = lax.rem(j * part + width - EDGE, width) + lax.broadcasted_iota(jnp.int32, (1, window), 1)
    column = jnp.where(column >= width, column - width, column)
    before = jnp.where(column == 0, width - 1, column - 1)
    after = jnp.where(column == width - 1, 0, column + 1)

    def choice(ref):
        table = jnp.concatenate([ref[:, across(j, q)] for q in range(PIECES)], axis=1)
        return jnp.where(table == column, 1, jnp.where(table == before, 2, jnp.where(table == after, 3, 0)))

    top = choice(top_ref)
    bottom = choice(bottom_ref)

    def rims(k):
        @pl.when(has_above)
        def _():
            for q in range(PIECES):
                up_copy(k, q).wait_recv()

        @pl.when(has_below)
        def _():
            for q in range(PIECES):
                low_copy(k, q).wait_recv()

        padded[0, source(k)] = remap(upper[source(k)], jnp.broadcast_to(top, (c, window)))
        padded[3, source(k)] = remap(lower[source(k)], jnp.broadcast_to(bottom, (c, window)))

    for q in range(PIECES):
        for k in range(1, chan):
            x_copy(k, q).wait_recv()
            pass_on(k, q)

    def arrived(w, a, k):
        w_copy(w, a, k).wait_recv()
        w_pass(w, a, k).start()

    each_weight(0, arrived, nothing)
    for k in range(chan):
        rims(k)
    each_weight(0, nothing, lambda w, a, k: w_pass(w, a, k).wait_recv())
    for k in range(1, chan):
        b_copy(0, k).wait_recv()
        b_copy(1, k).wait_recv()
    for a in range(3):
        w_own(0, a).wait()
    bias = jnp.concatenate([as_column(b1_all[d]) for d in range(chan)], axis=0)

    def rim_copy():
        return remote(hid.at[1], rim, rim_send, rim_recv, (s + 1, j))

    def h_copy(r, k):
        mine = pl.ds(pl.multiple_of(j * part, EDGE), part)
        return remote(
            hid.at[r, peer(k), :, EDGE : EDGE + part], hidden_ref.at[r, :, mine],
            h_send.at[r, k], h_recv.at[r, k], (s, peer(k)),
        )

    spot = lax.broadcasted_iota(jnp.int32, (SPREAD, SPREAD), 0)
    wanted = lax.broadcasted_iota(jnp.int32, (SPREAD, SPREAD), 1)
    wanted = jnp.where(wanted < SPREAD // 2, 2 * wanted, 2 * wanted - SPREAD + 1)
    picker = jnp.where(spot == wanted, 1.0, 0.0).astype(BF16)

    def split_columns(row, at):
        odd[at, :, :EDGE] = row[:, :EDGE]
        for block in range(part // SPREAD):
            first = EDGE + block * SPREAD
            both = jnp.dot(row[:, first : first + SPREAD], picker, preferred_element_type=F32).astype(BF16)
            here = block * (SPREAD // 2)
            even[at, :, here : here + SPREAD // 2] = both[:, : SPREAD // 2]
            odd[at, :, EDGE + here : EDGE + here + SPREAD // 2] = both[:, SPREAD // 2 :]

    taps = wide1[...].reshape(3 * channels, 3 * channels)
    for r in (1, 0):
        for first in range(0, window, SPREAD):
            stack = padded[r : r + 3, :, :, first : first + SPREAD].reshape(3 * channels, SPREAD)
            totals[:, first : first + SPREAD] = jnp.dot(taps, stack, preferred_element_type=F32)
        pre = (
            pltpu.roll(totals[:channels], 1, 1)
            + totals[channels : 2 * channels]
            + pltpu.roll(totals[2 * channels :], window - 1, 1)
            + bias
        )
        hid[r] = gelu(pre).astype(BF16).reshape(chan, o, window)
        if r == 1:
            @pl.when(has_below)
            def _():
                rim_copy().start()
        for k in range(1, chan):
            h_copy(r, k).start()

    own = pl.ds(pl.multiple_of(j * part, EDGE), part)
    hidden_ref[:, :, own] = hid[:, j, :, EDGE : EDGE + part]
    split_columns(hid[0].reshape(channels, window), 1)
    split_columns(hid[1].reshape(channels, window), 2)
    each_weight(1, arrived, nothing)
    each_weight(1, nothing, lambda w, a, k: w_pass(w, a, k).wait_recv())
    for a in range(3):
        w_own(1, a).wait()

    def convolved(owner, first, last):
        depth = (last - first) * channels
        lanes = slice(first * channels, last * channels)

        def product(b, data):
            return jnp.dot(wide2[b, owner, :, lanes], data, preferred_element_type=F32)

        evens = even[first:last].reshape(depth, half)
        odds = odd[first:last].reshape(depth, half + EDGE)
        shifted = pltpu.roll(product(0, odds), 1, 1)[:, EDGE:]
        return product(1, evens) + product(2, odds[:, EDGE:]) + shifted

    for k in range(chan):
        sums[k] = convolved(peer(k), 1, 3) + as_column(b2_all[peer(k)])

    @pl.when(has_above)
    def _():
        rim_copy().wait_recv()

    split_columns(remap(rim[...].reshape(channels, window), jnp.broadcast_to(top, (channels, window))), 0)

    def p_copy(k):
        mine = pl.ds(pl.multiple_of(j * half, EDGE), half)
        return remote(result.at[k], coarse_ref.at[:, mine], p_send.at[k], p_recv.at[k], (s, peer(k)))

    for k in range(1, chan):
        result[k] = gelu(sums[k] + convolved(peer(k), 0, 1)).astype(BF16)
        p_copy(k).start()
    ours = pl.ds(pl.multiple_of(j * half, EDGE), half)
    coarse_ref[:, ours] = gelu(sums[0] + convolved(j, 0, 1)).astype(BF16)

    for k in range(1, chan):
        for q in range(PIECES):
            x_copy(k, q).wait_send()
        for which in range(2):
            b_copy(which, k).wait_send()
        for r in range(2):
            h_copy(r, k).wait()
        p_copy(k).wait()

    def sent(w, a, k):
        w_copy(w, a, k).wait_send()
        w_pass(w, a, k).wait_send()

    each_weight(0, sent, nothing)
    each_weight(1, sent, nothing)

    @pl.when(has_below)
    def _():
        for k in range(chan):
            for q in range(PIECES):
                up_copy(k, q).wait_send()
        rim_copy().wait_send()

    @pl.when(has_above)
    def _():
        for k in range(chan):
            for q in range(PIECES):
                low_copy(k, q).wait_send()


def per_device(space, chan, features, top_map, bottom_map, first_weight, first_bias, second_weight, second_bias):
    _, c, rows, width = features.shape
    o, _, _, channels = first_weight.shape
    o2 = second_weight.shape[0]
    part = width // chan
    window = part + 2 * EDGE
    half = part // 2
    x = jnp.transpose(features[0], (1, 0, 2))
    w1 = jnp.transpose(first_weight, (1, 2, 0, 3))
    w2 = jnp.transpose(second_weight, (1, 2, 0, 3))
    dma = pltpu.SemaphoreType.DMA
    in_vmem = pl.BlockSpec(memory_space=pltpu.VMEM)
    anywhere = pl.BlockSpec(memory_space=pl.ANY)
    hidden, coarse = pl.pallas_call(
        functools.partial(kernel, space, chan),
        out_shape=(
            jax.ShapeDtypeStruct((rows, o, width), BF16),
            jax.ShapeDtypeStruct((o2, width // 2), BF16),
        ),
        in_specs=[in_vmem, in_vmem, in_vmem, anywhere, in_vmem, anywhere, in_vmem],
        out_specs=(in_vmem, in_vmem),
        scratch_shapes=[
            pltpu.VMEM((4, chan, c, window), BF16),
            pltpu.VMEM((chan, c, window), BF16),
            pltpu.VMEM((chan, c, window), BF16),
            pltpu.VMEM((3, chan, o, 3 * channels), BF16),
            pltpu.VMEM((3, chan, o2, 3 * channels), BF16),
            pltpu.VMEM((chan, 1, o), F32),
            pltpu.VMEM((chan, 1, o2), F32),
            pltpu.VMEM((3 * channels, window), F32),
            pltpu.VMEM((2, chan, o, window), BF16),
            pltpu.VMEM((chan, o, window), BF16),
            pltpu.VMEM((3, channels, half), BF16),
            pltpu.VMEM((3, channels, EDGE + half), BF16),
            pltpu.VMEM((chan, o2, half), F32),
            pltpu.VMEM((chan, o2, half), BF16),
            dma((chan, PIECES)),
            dma((chan, PIECES)),
            dma((chan, PIECES)),
            dma((chan, PIECES)),
            dma((chan, PIECES)),
            dma((chan, PIECES)),
            dma,
            dma,
            dma((2, 3)),
            dma((2, 3, chan)),
            dma((2, 3, chan)),
            dma((2, 3, chan)),
            dma((2, 3, chan)),
            dma((2, chan)),
            dma((2, chan)),
            dma((2, chan)),
            dma((2, chan)),
            dma((chan,)),
            dma((chan,)),
        ],
        compiler_params=pltpu.CompilerParams(
            collective_id=0, has_side_effects=True, vmem_limit_bytes=40 * 1024 * 1024
        ),
    )(x, top_map, bottom_map, w1, first_bias[None, :], w2, second_bias[None, :])
    return jnp.transpose(hidden, (1, 0, 2))[None], coarse[None, :, None, :]


def solution(mesh):
    placed = (
        P(None, "chan", "space", None),
        P("space", None),
        P("space", None),
        P("chan", None, None, None),
        P("chan"),
        P("chan", None, None, None),
        P("chan"),
    )
    return jax.shard_map(
        functools.partial(per_device, mesh.shape["space"], mesh.shape["chan"]),
        mesh=mesh,
        in_specs=placed,
        out_specs=(P(None, "chan", "space", None), P(None, "chan", "space", None)),
        check_vma=False,
    )
```

profile of v0, /device:TPU:0, one launch (start us, length us, event | category | flops | bytes accessed | tf_op | source)
XLA Modules:
  0.0 32.6 jit_solution(1815209664156121128)
XLA Ops:
  0.6 0.0 copy-start
  0.6 0.0 copy-start.1
  0.7 0.0 copy-start.2
  0.7 0.0 copy-start.3
  0.7 1.2 %copy.12 = bf16[1,64,2,2048]{3,1,2,0:T(8,128)(2,1)S(1)} copy(bf16[1,64,2,2048]{3,2,1,0:T(2,128)(2,1)} %param.7) | data formatting | bytes 1048576 | tf_op args[0]
  1.9 0.0 copy-start.4
  1.9 0.0 copy-start.5
  1.9 0.0 copy-done
  2.0 0.0 copy-done.1
  2.0 0.0 copy-done.2
  2.0 0.0 copy-done.3
  2.0 0.6 %copy-done.4 = f32[64]{0:T(128)S(1)} copy-done((f32[64]{0:T(128)S(1)}, f32[64]{0:T(128)}, u32[]{:S(2)}) %copy-start.4) | copy-done | bytes 280
  2.6 0.0 copy-done.5
  2.6 28.0 %shard_map.86 = (bf16[2,64,2048]{2,1,0:T(8,128)(2,1)S(1)}, bf16[128,1024]{1,0:T(8,128)(2,1)S(1)}) custom-call(bf16[2,64,2048]{2,1,0:T(8,128)(2,1)S(1)} %bitcast.13, s32[1,2048]{1,0:T(1,128)S(1)} %copy-done.2, s32[1,2048]{1,0:T(1,128)S(1)} %copy-done.3, bf16[3,3,64,128]{3,2,1,0:T(8,128)(2,1)S(1)} %bitcast.17, f32[1,64]{1,0:T(1,128)S(1)} %bitcast.18, ...), custom_call_target="tpu_custom_call" | custom-call | tf_op jit(solution)/shard_map/pallas_call | solution.py:355
  30.6 1.3 %copy.10 = bf16[1,64,2,2048]{3,2,1,0:T(2,128)(2,1)} copy(bf16[1,64,2,2048]{3,1,2,0:T(8,128)(2,1)S(1)} %bitcast.14) | data formatting | bytes 1048576
  31.9 0.7 %copy.14 = bf16[1,128,1,1024]{3,1,2,0:T(8,128)(2,1)} copy(bf16[1,128,1,1024]{3,1,2,0:T(8,128)(2,1)S(1)} %bitcast.16) | data formatting | bytes 524288
Async XLA Ops:
  0.6 1.3 %copy-start = (bf16[128,3,3,128]{3,0,2,1:T(8,128)(2,1)S(1)}, bf16[128,3,3,128]{3,0,2,1:T(8,128)(2,1)}, u32[]{:S(2)}) copy-start(bf16[128,3,3,128]{3,0,2,1:T(8,128)(2,1)} %param.12) | copy-start | bytes 884740
  0.6 1.3 %copy-start.1 = (bf16[64,3,3,128]{3,0,2,1:T(8,128)(2,1)S(1)}, bf16[64,3,3,128]{3,0,2,1:T(8,128)(2,1)}, u32[]{:S(2)}) copy-start(bf16[64,3,3,128]{3,0,2,1:T(8,128)(2,1)} %param.10) | copy-start | bytes 442372
  0.7 1.3 %copy-start.2 = (s32[1,2048]{1,0:T(1,128)S(1)}, s32[1,2048]{1,0:T(1,128)}, u32[]{:S(2)}) copy-start(s32[1,2048]{1,0:T(1,128)} %top_ref.1) | copy-start | bytes 24580
  0.7 1.3 %copy-start.3 = (s32[1,2048]{1,0:T(1,128)S(1)}, s32[1,2048]{1,0:T(1,128)}, u32[]{:S(2)}) copy-start(s32[1,2048]{1,0:T(1,128)} %bottom_ref.1) | copy-start | bytes 24580
  1.9 0.7 %copy-start.4 = (f32[64]{0:T(128)S(1)}, f32[64]{0:T(128)}, u32[]{:S(2)}) copy-start(f32[64]{0:T(128)} %param.11) | copy-start | bytes 772
  1.9 0.7 %copy-start.5 = (f32[128]{0:T(128)S(1)}, f32[128]{0:T(128)}, u32[]{:S(2)}) copy-start(f32[128]{0:T(128)} %param.13) | copy-start | bytes 1540
where the time goes:
time: 32.8 us; the launch traced here: 32.6 us
  Pallas kernels  28 us (85%)
  local copies, waits for them, and re-layouts  3.92 us (12%)
  between operations  0.72 us (2%)
    pallas_call x1, Pallas kernels, per_device(): pl.pallas_call(functools.partial(kernel, space, chan), out_shape=(jax.Sha...  28 us
    unnamed x15, local copies, waits for them, and re-layouts  3.92 us

commit v1 on v0

--- a/solution.py
+++ b/solution.py
@@ -13,6 +13,7 @@
 EDGE = 128
 SPREAD = 256
 PIECES = 4
+GROUP = 16
 
 
 def gelu(v):
@@ -27,6 +28,12 @@
     return found.astype(BF16)
 
 
+def remap_into(dst, src, pick):
+    for g in range(0, src.shape[0], GROUP):
+        rows = slice(g, g + GROUP)
+        dst[rows] = remap(src[rows], jnp.broadcast_to(pick, (GROUP, pick.shape[1])))
+
+
 def as_column(row):
     count = row.shape[1]
     down = lax.broadcasted_iota(jnp.int32, (count, count), 0)
@@ -36,7 +43,8 @@
 
 def kernel(
     space, chan, x_ref, top_ref, bottom_ref, w1_ref, b1_ref, w2_ref, b2_ref, hidden_ref, coarse_ref,
-    padded, upper, lower, wide1, wide2, b1_all, b2_all, totals, hid, rim, even, odd, sums, result,
+    padded, upper, lower, wide1, wide2, b1_all, b2_all, bias1, bias2, totals, hid, rim, fixed, even, odd,
+    sums, behind, result,
     x_send, x_recv, up_send, up_recv, low_send, low_recv, rim_send, rim_recv,
     own_sem, w_send, w_recv, f_send, f_recv, b_send, b_recv, h_send, h_recv, p_send, p_recv,
 ):
@@ -164,7 +172,6 @@
         b_copy(0, k).start()
         b_copy(1, k).start()
     each_weight(0, lambda w, a, k: w_copy(w, a, k).start(), nothing)
-    each_weight(1, lambda w, a, k: w_copy(w, a, k).start(), nothing)
 
     for q in range(PIECES):
         padded[1:3, j, :, there(q)] = x_ref[:, :, across(j, q)]
@@ -192,39 +199,55 @@
     top = choice(top_ref)
     bottom = choice(bottom_ref)
 
-    def rims(k):
+    def upper_rim(k):
         @pl.when(has_above)
         def _():
             for q in range(PIECES):
                 up_copy(k, q).wait_recv()
 
+        remap_into(padded.at[0, source(k)], upper.at[source(k)], top)
+
+    def lower_rim(k):
         @pl.when(has_below)
         def _():
             for q in range(PIECES):
                 low_copy(k, q).wait_recv()
 
-        padded[0, source(k)] = remap(upper[source(k)], jnp.broadcast_to(top, (c, window)))
-        padded[3, source(k)] = remap(lower[source(k)], jnp.broadcast_to(bottom, (c, window)))
-
+        remap_into(padded.at[3, source(k)], lower.at[source(k)], bottom)
+
+    lower_rim(0)
+    upper_rim(0)
     for q in range(PIECES):
         for k in range(1, chan):
             x_copy(k, q).wait_recv()
             pass_on(k, q)
+    each_weight(1, lambda w, a, k: w_copy(w, a, k).start(), nothing)
 
     def arrived(w, a, k):
         w_copy(w, a, k).wait_recv()
         w_pass(w, a, k).start()
 
     each_weight(0, arrived, nothing)
-    for k in range(chan):
-        rims(k)
     each_weight(0, nothing, lambda w, a, k: w_pass(w, a, k).wait_recv())
+    for a in range(3):
+        w_own(0, a).wait()
     for k in range(1, chan):
         b_copy(0, k).wait_recv()
         b_copy(1, k).wait_recv()
-    for a in range(3):
-        w_own(0, a).wait()
-    bias = jnp.concatenate([as_column(b1_all[d]) for d in range(chan)], axis=0)
+    for d in range(chan):
+        bias1[d * o : (d + 1) * o] = as_column(b1_all[d])
+        bias2[d * o2 : (d + 1) * o2] = as_column(b2_all[d])
+
+    def taps(first, last):
+        return wide1[:, :, :, first * channels : last * channels].reshape(3 * channels, (last - first) * channels)
+
+    def rows(first, last, at):
+        return padded[first:last, :, :, at : at + SPREAD].reshape((last - first) * channels, SPREAD)
+
+    for at in range(0, window, SPREAD):
+        inner = rows(1, 3, at)
+        for r in (1, 0):
+            totals[r, :, at : at + SPREAD] = jnp.dot(taps(1 - r, 3 - r), inner, preferred_element_type=F32)
 
     def rim_copy():
         return remote(hid.at[1], rim, rim_send, rim_recv, (s + 1, j))
@@ -250,18 +273,20 @@
             even[at, :, here : here + SPREAD // 2] = both[:, : SPREAD // 2]
             odd[at, :, EDGE + here : EDGE + here + SPREAD // 2] = both[:, SPREAD // 2 :]
 
-    taps = wide1[...].reshape(3 * channels, 3 * channels)
     for r in (1, 0):
-        for first in range(0, window, SPREAD):
-            stack = padded[r : r + 3, :, :, first : first + SPREAD].reshape(3 * channels, SPREAD)
-            totals[:, first : first + SPREAD] = jnp.dot(taps, stack, preferred_element_type=F32)
-        pre = (
-            pltpu.roll(totals[:channels], 1, 1)
-            + totals[channels : 2 * channels]
-            + pltpu.roll(totals[2 * channels :], window - 1, 1)
-            + bias
-        )
-        hid[r] = gelu(pre).astype(BF16).reshape(chan, o, window)
+        for k in range(1, chan):
+            lower_rim(k) if r == 1 else upper_rim(k)
+        for at in range(0, window, SPREAD):
+            outer = rows(3 * r, 3 * r + 1, at)
+            totals[r, :, at : at + SPREAD] += jnp.dot(taps(2 * r, 2 * r + 1), outer, preferred_element_type=F32)
+        for g in range(0, channels, GROUP):
+            pre = (
+                pltpu.roll(totals[r, g : g + GROUP], 1, 1)
+                + totals[r, channels + g : channels + g + GROUP]
+                + pltpu.roll(totals[r, 2 * channels + g : 2 * channels + g + GROUP], window - 1, 1)
+                + bias1[g : g + GROUP]
+            )
+            hid[r, g // o, g % o : g % o + GROUP] = gelu(pre).astype(BF16)
         if r == 1:
             @pl.when(has_below)
             def _():
@@ -278,36 +303,44 @@
     for a in range(3):
         w_own(1, a).wait()
 
-    def convolved(owner, first, last):
+    def products(first, last):
         depth = (last - first) * channels
         lanes = slice(first * channels, last * channels)
 
         def product(b, data):
-            return jnp.dot(wide2[b, owner, :, lanes], data, preferred_element_type=F32)
-
-        evens = even[first:last].reshape(depth, half)
+            weight = wide2[b, :, :, lanes].reshape(chan * o2, depth)
+            return jnp.dot(weight, data, preferred_element_type=F32)
+
         odds = odd[first:last].reshape(depth, half + EDGE)
-        shifted = pltpu.roll(product(0, odds), 1, 1)[:, EDGE:]
-        return product(1, evens) + product(2, odds[:, EDGE:]) + shifted
-
-    for k in range(chan):
-        sums[k] = convolved(peer(k), 1, 3) + as_column(b2_all[peer(k)])
+        behind[...] = product(0, odds)
+        return product(1, even[first:last].reshape(depth, half)) + product(2, odds[:, EDGE:])
+
+    def shifted(g):
+        return pltpu.roll(behind[g : g + GROUP], 1, 1)[:, EDGE:]
+
+    sums[...] = products(1, 3)
+    for g in range(0, chan * o2, GROUP):
+        sums[g : g + GROUP] = sums[g : g + GROUP] + shifted(g) + bias2[g : g + GROUP]
 
     @pl.when(has_above)
     def _():
         rim_copy().wait_recv()
 
-    split_columns(remap(rim[...].reshape(channels, window), jnp.broadcast_to(top, (channels, window))), 0)
+    for d in range(chan):
+        remap_into(fixed.at[d], rim.at[d], top)
+    split_columns(fixed[...].reshape(channels, window), 0)
+    sums[...] += products(0, 1)
 
     def p_copy(k):
         mine = pl.ds(pl.multiple_of(j * half, EDGE), half)
-        return remote(result.at[k], coarse_ref.at[:, mine], p_send.at[k], p_recv.at[k], (s, peer(k)))
-
+        return remote(result.at[peer(k)], coarse_ref.at[:, mine], p_send.at[k], p_recv.at[k], (s, peer(k)))
+
+    for g in range(0, chan * o2, GROUP):
+        result[g // o2, g % o2 : g % o2 + GROUP] = gelu(sums[g : g + GROUP] + shifted(g)).astype(BF16)
     for k in range(1, chan):
-        result[k] = gelu(sums[k] + convolved(peer(k), 0, 1)).astype(BF16)
         p_copy(k).start()
     ours = pl.ds(pl.multiple_of(j * half, EDGE), half)
-    coarse_ref[:, ours] = gelu(sums[0] + convolved(j, 0, 1)).astype(BF16)
+    coarse_ref[:, ours] = result[j]
 
     for k in range(1, chan):
         for q in range(PIECES):
@@ -351,14 +384,14 @@
     w2 = jnp.transpose(second_weight, (1, 2, 0, 3))
     dma = pltpu.SemaphoreType.DMA
     in_vmem = pl.BlockSpec(memory_space=pltpu.VMEM)
-    anywhere = pl.BlockSpec(memory_space=pl.ANY)
+    in_hbm = pl.BlockSpec(memory_space=pltpu.HBM)
     hidden, coarse = pl.pallas_call(
         functools.partial(kernel, space, chan),
         out_shape=(
             jax.ShapeDtypeStruct((rows, o, width), BF16),
             jax.ShapeDtypeStruct((o2, width // 2), BF16),
         ),
-        in_specs=[in_vmem, in_vmem, in_vmem, anywhere, in_vmem, anywhere, in_vmem],
+        in_specs=[in_vmem, in_vmem, in_vmem, in_hbm, in_vmem, in_hbm, in_vmem],
         out_specs=(in_vmem, in_vmem),
         scratch_shapes=[
             pltpu.VMEM((4, chan, c, window), BF16),
@@ -368,12 +401,16 @@
             pltpu.VMEM((3, chan, o2, 3 * channels), BF16),
             pltpu.VMEM((chan, 1, o), F32),
             pltpu.VMEM((chan, 1, o2), F32),
-            pltpu.VMEM((3 * channels, window), F32),
+            pltpu.VMEM((channels, 1), F32),
+            pltpu.VMEM((chan * o2, 1), F32),
+            pltpu.VMEM((2, 3 * channels, window), F32),
             pltpu.VMEM((2, chan, o, window), BF16),
+            pltpu.VMEM((chan, o, window), BF16),
             pltpu.VMEM((chan, o, window), BF16),
             pltpu.VMEM((3, channels, half), BF16),
             pltpu.VMEM((3, channels, EDGE + half), BF16),
-            pltpu.VMEM((chan, o2, half), F32),
+            pltpu.VMEM((chan * o2, half), F32),
+            pltpu.VMEM((chan * o2, EDGE + half), F32),
             pltpu.VMEM((chan, o2, half), BF16),
             dma((chan, PIECES)),
             dma((chan, PIECES)),

time: 32.8 us -> 31.5 us (0.960)
  Pallas kernels: 28 us -> 26.6 us
    pallas_call x1, Pallas kernels: 28 us -> 26.6 us  [per_device(): pl.pallas_call(functools.partial(kernel, space, chan), out_shape=(jax.Sha...]
where the time goes in v1:
time: 31.5 us; the launch traced here: 31.3 us
  Pallas kernels  26.6 us (84%)
  local copies, waits for them, and re-layouts  3.92 us (12%)
  between operations  0.72 us (2%)
    pallas_call x1, Pallas kernels, per_device(): pl.pallas_call(functools.partial(kernel, space, chan), out_shape=(jax.Sha...  26.6 us
    unnamed x15, local copies, waits for them, and re-layouts  3.92 us

profile of v1, /device:TPU:0, one launch (start us, length us, event | category | flops | bytes accessed | tf_op | source)
XLA Modules:
  0.0 31.3 jit_solution(7940546997671587721)
XLA Ops:
  0.6 0.0 copy-start
  0.6 0.0 copy-start.1
  0.7 0.0 copy-start.2
  0.7 0.0 copy-start.3
  0.7 1.2 %copy.12 = bf16[1,64,2,2048]{3,1,2,0:T(8,128)(2,1)S(1)} copy(bf16[1,64,2,2048]{3,2,1,0:T(2,128)(2,1)} %param.7) | data formatting | bytes 1048576 | tf_op args[0]
  1.9 0.0 copy-start.4
  1.9 0.0 copy-start.5
  1.9 0.0 copy-done
  2.0 0.0 copy-done.1
  2.0 0.0 copy-done.2
  2.0 0.0 copy-done.3
  2.0 0.6 %copy-done.4 = f32[64]{0:T(128)S(1)} copy-done((f32[64]{0:T(128)S(1)}, f32[64]{0:T(128)}, u32[]{:S(2)}) %copy-start.4) | copy-done | bytes 280
  2.6 0.0 copy-done.5
  2.6 26.6 %shard_map.86 = (bf16[2,64,2048]{2,1,0:T(8,128)(2,1)S(1)}, bf16[128,1024]{1,0:T(8,128)(2,1)S(1)}) custom-call(bf16[2,64,2048]{2,1,0:T(8,128)(2,1)S(1)} %bitcast.13, s32[1,2048]{1,0:T(1,128)S(1)} %copy-done.2, s32[1,2048]{1,0:T(1,128)S(1)} %copy-done.3, bf16[3,3,64,128]{3,2,1,0:T(8,128)(2,1)S(1)} %bitcast.17, f32[1,64]{1,0:T(1,128)S(1)} %bitcast.18, ...), custom_call_target="tpu_custom_call" | custom-call | tf_op jit(solution)/shard_map/pallas_call | solution.py:388
  29.3 1.3 %copy.10 = bf16[1,64,2,2048]{3,2,1,0:T(2,128)(2,1)} copy(bf16[1,64,2,2048]{3,1,2,0:T(8,128)(2,1)S(1)} %bitcast.14) | data formatting | bytes 1048576
  30.6 0.7 %copy.14 = bf16[1,128,1,1024]{3,1,2,0:T(8,128)(2,1)} copy(bf16[1,128,1,1024]{3,1,2,0:T(8,128)(2,1)S(1)} %bitcast.16) | data formatting | bytes 524288
Async XLA Ops:
  0.6 1.3 %copy-start = (bf16[128,3,3,128]{3,0,2,1:T(8,128)(2,1)S(1)}, bf16[128,3,3,128]{3,0,2,1:T(8,128)(2,1)}, u32[]{:S(2)}) copy-start(bf16[128,3,3,128]{3,0,2,1:T(8,128)(2,1)} %param.12) | copy-start | bytes 884740
  0.6 1.3 %copy-start.1 = (bf16[64,3,3,128]{3,0,2,1:T(8,128)(2,1)S(1)}, bf16[64,3,3,128]{3,0,2,1:T(8,128)(2,1)}, u32[]{:S(2)}) copy-start(bf16[64,3,3,128]{3,0,2,1:T(8,128)(2,1)} %param.10) | copy-start | bytes 442372
  0.7 1.3 %copy-start.2 = (s32[1,2048]{1,0:T(1,128)S(1)}, s32[1,2048]{1,0:T(1,128)}, u32[]{:S(2)}) copy-start(s32[1,2048]{1,0:T(1,128)} %top_ref.1) | copy-start | bytes 24580
  0.7 1.3 %copy-start.3 = (s32[1,2048]{1,0:T(1,128)S(1)}, s32[1,2048]{1,0:T(1,128)}, u32[]{:S(2)}) copy-start(s32[1,2048]{1,0:T(1,128)} %bottom_ref.1) | copy-start | bytes 24580
  1.9 0.7 %copy-start.4 = (f32[64]{0:T(128)S(1)}, f32[64]{0:T(128)}, u32[]{:S(2)}) copy-start(f32[64]{0:T(128)} %param.11) | copy-start | bytes 772
  1.9 0.7 %copy-start.5 = (f32[128]{0:T(128)S(1)}, f32[128]{0:T(128)}, u32[]{:S(2)}) copy-start(f32[128]{0:T(128)} %param.13) | copy-start | bytes 1540

commit v2 on v1

--- a/solution.py
+++ b/solution.py
@@ -43,9 +43,9 @@
 
 def kernel(
     space, chan, x_ref, top_ref, bottom_ref, w1_ref, b1_ref, w2_ref, b2_ref, hidden_ref, coarse_ref,
-    padded, upper, lower, wide1, wide2, b1_all, b2_all, bias1, bias2, totals, hid, rim, fixed, even, odd,
+    padded, upper, lower, wide1, wide2, b1_all, b2_all, bias1, bias2, totals, hid, joint, table_above, fixed, even, odd,
     sums, behind, result,
-    x_send, x_recv, up_send, up_recv, low_send, low_recv, rim_send, rim_recv,
+    x_send, x_recv, up_send, up_recv, low_send, low_recv, t_send, t_recv,
     own_sem, w_send, w_recv, f_send, f_recv, b_send, b_recv, h_send, h_recv, p_send, p_recv,
 ):
     s = lax.axis_index("space")
@@ -101,12 +101,15 @@
         )
 
     def up_copy(k, q):
-        src = x_ref.at[1, :, across(j, q)] if k == 0 else padded.at[2, source(k), :, there(q)]
-        return remote(src, upper.at[source(k), :, there(q)], up_send.at[k, q], up_recv.at[k, q], (s + 1, j))
+        src = x_ref.at[:, :, across(j, q)] if k == 0 else padded.at[1:3, source(k), :, there(q)]
+        return remote(src, upper.at[:, source(k), :, there(q)], up_send.at[k, q], up_recv.at[k, q], (s + 1, j))
 
     def low_copy(k, q):
         src = x_ref.at[0, :, across(j, q)] if k == 0 else padded.at[1, source(k), :, there(q)]
         return remote(src, lower.at[source(k), :, there(q)], low_send.at[k, q], low_recv.at[k, q], (s - 1, j))
+
+    def table_copy():
+        return remote(bottom_ref, table_above, t_send, t_recv, (s + 1, j))
 
     def pass_on(k, q):
         @pl.when(has_below)
@@ -171,6 +174,11 @@
     for k in range(1, chan):
         b_copy(0, k).start()
         b_copy(1, k).start()
+
+    @pl.when(has_below)
+    def _():
+        table_copy().start()
+
     each_weight(0, lambda w, a, k: w_copy(w, a, k).start(), nothing)
 
     for q in range(PIECES):
@@ -181,7 +189,7 @@
     @pl.when(s == 0)
     def _():
         upper[...] = jnp.zeros_like(upper)
-        rim[...] = jnp.zeros_like(rim)
+        table_above[...] = jnp.zeros_like(table_above)
 
     @pl.when(s == space - 1)
     def _():
@@ -196,7 +204,7 @@
         table = jnp.concatenate([ref[:, across(j, q)] for q in range(PIECES)], axis=1)
         return jnp.where(table == column, 1, jnp.where(table == before, 2, jnp.where(table == after, 3, 0)))
 
-    top = choice(top_ref)
+    top = jnp.where(has_above, choice(top_ref), 0)
     bottom = choice(bottom_ref)
 
     def upper_rim(k):
@@ -205,7 +213,7 @@
             for q in range(PIECES):
                 up_copy(k, q).wait_recv()
 
-        remap_into(padded.at[0, source(k)], upper.at[source(k)], top)
+        remap_into(padded.at[0, source(k)], upper.at[1, source(k)], top)
 
     def lower_rim(k):
         @pl.when(has_below)
@@ -217,6 +225,13 @@
 
     lower_rim(0)
     upper_rim(0)
+
+    @pl.when(has_above)
+    def _():
+        table_copy().wait_recv()
+
+    above = choice(table_above)
+    remap_into(joint.at[j], padded.at[1, j], above)
     for q in range(PIECES):
         for k in range(1, chan):
             x_copy(k, q).wait_recv()
@@ -228,6 +243,8 @@
         w_pass(w, a, k).start()
 
     each_weight(0, arrived, nothing)
+    for k in range(1, chan):
+        remap_into(joint.at[source(k)], padded.at[1, source(k)], above)
     each_weight(0, nothing, lambda w, a, k: w_pass(w, a, k).wait_recv())
     for a in range(3):
         w_own(0, a).wait()
@@ -244,13 +261,17 @@
     def rows(first, last, at):
         return padded[first:last, :, :, at : at + SPREAD].reshape((last - first) * channels, SPREAD)
 
+    def outer(r, at):
+        if r == 2:
+            return upper[:, :, :, at : at + SPREAD].reshape(2 * channels, SPREAD)
+        return rows(3 * r, 3 * r + 1, at)
+
     for at in range(0, window, SPREAD):
         inner = rows(1, 3, at)
         for r in (1, 0):
             totals[r, :, at : at + SPREAD] = jnp.dot(taps(1 - r, 3 - r), inner, preferred_element_type=F32)
-
-    def rim_copy():
-        return remote(hid.at[1], rim, rim_send, rim_recv, (s + 1, j))
+        below = joint[:, :, at : at + SPREAD].reshape(channels, SPREAD)
+        totals[2, :, at : at + SPREAD] = jnp.dot(taps(2, 3), below, preferred_element_type=F32)
 
     def h_copy(r, k):
         mine = pl.ds(pl.multiple_of(j * part, EDGE), part)
@@ -273,12 +294,15 @@
             even[at, :, here : here + SPREAD // 2] = both[:, : SPREAD // 2]
             odd[at, :, EDGE + here : EDGE + here + SPREAD // 2] = both[:, SPREAD // 2 :]
 
-    for r in (1, 0):
+    for r in (1, 0, 2):
         for k in range(1, chan):
-            lower_rim(k) if r == 1 else upper_rim(k)
+            if r == 1:
+                lower_rim(k)
+            if r == 0:
+                upper_rim(k)
+        outer_taps = (taps(0, 1), taps(2, 3), taps(0, 2))[r]
         for at in range(0, window, SPREAD):
-            outer = rows(3 * r, 3 * r + 1, at)
-            totals[r, :, at : at + SPREAD] += jnp.dot(taps(2 * r, 2 * r + 1), outer, preferred_element_type=F32)
+            totals[r, :, at : at + SPREAD] += jnp.dot(outer_taps, outer(r, at), preferred_element_type=F32)
         for g in range(0, channels, GROUP):
             pre = (
                 pltpu.roll(totals[r, g : g + GROUP], 1, 1)
@@ -286,18 +310,20 @@
                 + pltpu.roll(totals[r, 2 * channels + g : 2 * channels + g + GROUP], window - 1, 1)
                 + bias1[g : g + GROUP]
             )
-            hid[r, g // o, g % o : g % o + GROUP] = gelu(pre).astype(BF16)
-        if r == 1:
-            @pl.when(has_below)
-            def _():
-                rim_copy().start()
-        for k in range(1, chan):
-            h_copy(r, k).start()
+            row = gelu(pre).astype(BF16)
+            if r == 2:
+                fixed[g : g + GROUP] = remap(row, jnp.broadcast_to(top, (GROUP, window)))
+            else:
+                hid[r, g // o, g % o : g % o + GROUP] = row
+        if r < 2:
+            for k in range(1, chan):
+                h_copy(r, k).start()
 
     own = pl.ds(pl.multiple_of(j * part, EDGE), part)
     hidden_ref[:, :, own] = hid[:, j, :, EDGE : EDGE + part]
     split_columns(hid[0].reshape(channels, window), 1)
     split_columns(hid[1].reshape(channels, window), 2)
+    split_columns(fixed[...], 0)
     each_weight(1, arrived, nothing)
     each_weight(1, nothing, lambda w, a, k: w_pass(w, a, k).wait_recv())
     for a in range(3):
@@ -315,32 +341,29 @@
         behind[...] = product(0, odds)
         return product(1, even[first:last].reshape(depth, half)) + product(2, odds[:, EDGE:])
 
-    def shifted(g):
-        return pltpu.roll(behind[g : g + GROUP], 1, 1)[:, EDGE:]
-
-    sums[...] = products(1, 3)
-    for g in range(0, chan * o2, GROUP):
-        sums[g : g + GROUP] = sums[g : g + GROUP] + shifted(g) + bias2[g : g + GROUP]
-
-    @pl.when(has_above)
-    def _():
-        rim_copy().wait_recv()
-
-    for d in range(chan):
-        remap_into(fixed.at[d], rim.at[d], top)
-    split_columns(fixed[...].reshape(channels, window), 0)
-    sums[...] += products(0, 1)
-
-    def p_copy(k):
+    sums[...] = products(0, 3)
+    piece = o2 // 2
+
+    def p_copy(k, h):
         mine = pl.ds(pl.multiple_of(j * half, EDGE), half)
-        return remote(result.at[peer(k)], coarse_ref.at[:, mine], p_send.at[k], p_recv.at[k], (s, peer(k)))
-
-    for g in range(0, chan * o2, GROUP):
-        result[g // o2, g % o2 : g % o2 + GROUP] = gelu(sums[g : g + GROUP] + shifted(g)).astype(BF16)
-    for k in range(1, chan):
-        p_copy(k).start()
+        these = slice(h * piece, (h + 1) * piece)
+        return remote(
+            result.at[peer(k), these], coarse_ref.at[these, mine], p_send.at[k, h], p_recv.at[k, h], (s, peer(k))
+        )
+
     ours = pl.ds(pl.multiple_of(j * half, EDGE), half)
-    coarse_ref[:, ours] = result[j]
+    for k in [*range(1, chan), 0]:
+        for h in range(2):
+            for g in range(h * piece, (h + 1) * piece, GROUP):
+                at = pl.ds(pl.multiple_of(peer(k) * o2 + g, GROUP), GROUP)
+                shifted = pltpu.roll(behind[at], 1, 1)[:, EDGE:]
+                value = gelu(sums[at] + shifted + bias2[at]).astype(BF16)
+                if k == 0:
+                    coarse_ref[g : g + GROUP, ours] = value
+                else:
+                    result[peer(k), g : g + GROUP] = value
+            if k > 0:
+                p_copy(k, h).start()
 
     for k in range(1, chan):
         for q in range(PIECES):
@@ -349,7 +372,8 @@
             b_copy(which, k).wait_send()
         for r in range(2):
             h_copy(r, k).wait()
-        p_copy(k).wait()
+        for h in range(2):
+            p_copy(k, h).wait()
 
     def sent(w, a, k):
         w_copy(w, a, k).wait_send()
@@ -363,7 +387,7 @@
         for k in range(chan):
             for q in range(PIECES):
                 up_copy(k, q).wait_send()
-        rim_copy().wait_send()
+        table_copy().wait_send()
 
     @pl.when(has_above)
     def _():
@@ -395,7 +419,7 @@
         out_specs=(in_vmem, in_vmem),
         scratch_shapes=[
             pltpu.VMEM((4, chan, c, window), BF16),
-            pltpu.VMEM((chan, c, window), BF16),
+            pltpu.VMEM((2, chan, c, window), BF16),
             pltpu.VMEM((chan, c, window), BF16),
             pltpu.VMEM((3, chan, o, 3 * channels), BF16),
             pltpu.VMEM((3, chan, o2, 3 * channels), BF16),
@@ -403,10 +427,11 @@
             pltpu.VMEM((chan, 1, o2), F32),
             pltpu.VMEM((channels, 1), F32),
             pltpu.VMEM((chan * o2, 1), F32),
-            pltpu.VMEM((2, 3 * channels, window), F32),
+            pltpu.VMEM((3, 3 * channels, window), F32),
             pltpu.VMEM((2, chan, o, window), BF16),
-            pltpu.VMEM((chan, o, window), BF16),
-            pltpu.VMEM((chan, o, window), BF16),
+            pltpu.VMEM((chan, c, window), BF16),
+            pltpu.VMEM((1, width), jnp.int32),
+            pltpu.VMEM((channels, window), BF16),
             pltpu.VMEM((3, channels, half), BF16),
             pltpu.VMEM((3, channels, EDGE + half), BF16),
             pltpu.VMEM((chan * o2, half), F32),
@@ -429,8 +454,8 @@
             dma((2, chan)),
             dma((2, chan)),
             dma((2, chan)),
-            dma((chan,)),
-            dma((chan,)),
+            dma((chan, 2)),
+            dma((chan, 2)),
         ],
         compiler_params=pltpu.CompilerParams(
             collective_id=0, has_side_effects=True, vmem_limit_bytes=40 * 1024 * 1024

time: 31.5 us -> 32.1 us (1.019)
  Pallas kernels: 26.6 us -> 27.3 us
    pallas_call x1, Pallas kernels: 26.6 us -> 27.3 us  [per_device(): pl.pallas_call(functools.partial(kernel, space, chan), out_shape=(jax.Sha...]
where the time goes in v2:
time: 32.1 us; the launch traced here: 32 us
  Pallas kernels  27.3 us (85%)
  local copies, waits for them, and re-layouts  3.92 us (12%)
  between operations  0.72 us (2%)
    pallas_call x1, Pallas kernels, per_device(): pl.pallas_call(functools.partial(kernel, space, chan), out_shape=(jax.Sha...  27.3 us
    unnamed x15, local copies, waits for them, and re-layouts  3.92 us

profile of v2, /device:TPU:0, one launch (start us, length us, event | category | flops | bytes accessed | tf_op | source)
XLA Modules:
  0.0 32.0 jit_solution(9887957272724164416)
XLA Ops:
  0.6 0.0 copy-start
  0.6 0.0 copy-start.1
  0.7 0.0 copy-start.2
  0.7 0.0 copy-start.3
  0.7 1.2 %copy.12 = bf16[1,64,2,2048]{3,1,2,0:T(8,128)(2,1)S(1)} copy(bf16[1,64,2,2048]{3,2,1,0:T(2,128)(2,1)} %param.7) | data formatting | bytes 1048576 | tf_op args[0]
  1.9 0.0 copy-start.4
  1.9 0.0 copy-start.5
  1.9 0.0 copy-done
  2.0 0.0 copy-done.1
  2.0 0.0 copy-done.2
  2.0 0.0 copy-done.3
  2.0 0.6 %copy-done.4 = f32[64]{0:T(128)S(1)} copy-done((f32[64]{0:T(128)S(1)}, f32[64]{0:T(128)}, u32[]{:S(2)}) %copy-start.4) | copy-done | bytes 280
  2.6 0.0 copy-done.5
  2.6 27.3 %shard_map.86 = (bf16[2,64,2048]{2,1,0:T(8,128)(2,1)S(1)}, bf16[128,1024]{1,0:T(8,128)(2,1)S(1)}) custom-call(bf16[2,64,2048]{2,1,0:T(8,128)(2,1)S(1)} %bitcast.13, s32[1,2048]{1,0:T(1,128)S(1)} %copy-done.2, s32[1,2048]{1,0:T(1,128)S(1)} %copy-done.3, bf16[3,3,64,128]{3,2,1,0:T(8,128)(2,1)S(1)} %bitcast.17, f32[1,64]{1,0:T(1,128)S(1)} %bitcast.18, ...), custom_call_target="tpu_custom_call" | custom-call | tf_op jit(solution)/shard_map/pallas_call | solution.py:412
  29.9 1.3 %copy.10 = bf16[1,64,2,2048]{3,2,1,0:T(2,128)(2,1)} copy(bf16[1,64,2,2048]{3,1,2,0:T(8,128)(2,1)S(1)} %bitcast.14) | data formatting | bytes 1048576
  31.3 0.7 %copy.14 = bf16[1,128,1,1024]{3,1,2,0:T(8,128)(2,1)} copy(bf16[1,128,1,1024]{3,1,2,0:T(8,128)(2,1)S(1)} %bitcast.16) | data formatting | bytes 524288
Async XLA Ops:
  0.6 1.3 %copy-start = (bf16[128,3,3,128]{3,0,2,1:T(8,128)(2,1)S(1)}, bf16[128,3,3,128]{3,0,2,1:T(8,128)(2,1)}, u32[]{:S(2)}) copy-start(bf16[128,3,3,128]{3,0,2,1:T(8,128)(2,1)} %param.12) | copy-start | bytes 884740
  0.6 1.3 %copy-start.1 = (bf16[64,3,3,128]{3,0,2,1:T(8,128)(2,1)S(1)}, bf16[64,3,3,128]{3,0,2,1:T(8,128)(2,1)}, u32[]{:S(2)}) copy-start(bf16[64,3,3,128]{3,0,2,1:T(8,128)(2,1)} %param.10) | copy-start | bytes 442372
  0.7 1.3 %copy-start.2 = (s32[1,2048]{1,0:T(1,128)S(1)}, s32[1,2048]{1,0:T(1,128)}, u32[]{:S(2)}) copy-start(s32[1,2048]{1,0:T(1,128)} %top_ref.1) | copy-start | bytes 24580
  0.7 1.3 %copy-start.3 = (s32[1,2048]{1,0:T(1,128)S(1)}, s32[1,2048]{1,0:T(1,128)}, u32[]{:S(2)}) copy-start(s32[1,2048]{1,0:T(1,128)} %bottom_ref.1) | copy-start | bytes 24580
  1.9 0.7 %copy-start.4 = (f32[64]{0:T(128)S(1)}, f32[64]{0:T(128)}, u32[]{:S(2)}) copy-start(f32[64]{0:T(128)} %param.11) | copy-start | bytes 772
  1.9 0.7 %copy-start.5 = (f32[128]{0:T(128)S(1)}, f32[128]{0:T(128)}, u32[]{:S(2)}) copy-start(f32[128]{0:T(128)} %param.13) | copy-start | bytes 1540

commit v3 on v1

--- a/solution.py
+++ b/solution.py
@@ -12,7 +12,7 @@
 F32 = jnp.float32
 EDGE = 128
 SPREAD = 256
-PIECES = 4
+PIECES = 3
 GROUP = 16
 
 
@@ -43,7 +43,7 @@
 
 def kernel(
     space, chan, x_ref, top_ref, bottom_ref, w1_ref, b1_ref, w2_ref, b2_ref, hidden_ref, coarse_ref,
-    padded, upper, lower, wide1, wide2, b1_all, b2_all, bias1, bias2, totals, hid, rim, fixed, even, odd,
+    edge, padded, upper, lower, wide1, wide2, b1_all, b2_all, bias1, bias2, totals, hid, rim, fixed, even, odd,
     sums, behind, result,
     x_send, x_recv, up_send, up_recv, low_send, low_recv, rim_send, rim_recv,
     own_sem, w_send, w_recv, f_send, f_recv, b_send, b_recv, h_send, h_recv, p_send, p_recv,
@@ -55,7 +55,7 @@
     o = w1_ref.shape[2]
     o2 = w2_ref.shape[2]
     part = width // chan
-    window = part + 2 * EDGE
+    window = part + EDGE
     half = part // 2
     has_above = s > 0
     has_below = s < space - 1
@@ -85,27 +85,34 @@
     def _():
         pl.semaphore_signal(barrier, inc=1, device_id=(s + 1, j), device_id_type=MESH)
 
-    spans = ((0, EDGE), (EDGE, half), (EDGE + half, half), (EDGE + part, EDGE))
+    spans = ((0, EDGE), (EDGE, half), (EDGE + half, half))
 
     def there(q):
         return pl.ds(spans[q][0], spans[q][1])
 
     def across(owner, q):
-        begin = lax.rem(owner * part + width - EDGE + spans[q][0], width)
-        return pl.ds(pl.multiple_of(begin, EDGE), spans[q][1])
+        return pl.ds(pl.multiple_of(owner * part + (spans[q][0] - EDGE), EDGE), spans[q][1])
+
+    def edges(owner):
+        left = pl.ds(pl.multiple_of(lax.rem(owner * part + width - EDGE, width), EDGE), EDGE)
+        right = pl.ds(pl.multiple_of(lax.rem(owner * part + part, width), EDGE), EDGE)
+        return left, right
 
     def x_copy(k, q):
+        src = edge.at[peer(k)] if q == 0 else x_ref.at[:, :, across(peer(k), q)]
         return remote(
-            x_ref.at[:, :, across(peer(k), q)], padded.at[1:3, j, :, there(q)],
-            x_send.at[k, q], x_recv.at[k, q], (s, peer(k)),
-        )
+            src, padded.at[1:3, j, :, there(q)], x_send.at[k, q], x_recv.at[k, q], (s, peer(k)),
+        )
+
+    def own_row(r, q):
+        return edge.at[j, r] if q == 0 else x_ref.at[r, :, across(j, q)]
 
     def up_copy(k, q):
-        src = x_ref.at[1, :, across(j, q)] if k == 0 else padded.at[2, source(k), :, there(q)]
+        src = own_row(1, q) if k == 0 else padded.at[2, source(k), :, there(q)]
         return remote(src, upper.at[source(k), :, there(q)], up_send.at[k, q], up_recv.at[k, q], (s + 1, j))
 
     def low_copy(k, q):
-        src = x_ref.at[0, :, across(j, q)] if k == 0 else padded.at[1, source(k), :, there(q)]
+        src = own_row(0, q) if k == 0 else padded.at[1, source(k), :, there(q)]
         return remote(src, lower.at[source(k), :, there(q)], low_send.at[k, q], low_recv.at[k, q], (s - 1, j))
 
     def pass_on(k, q):
@@ -162,6 +169,12 @@
     for which in range(2):
         for a in range(3):
             w_own(which, a).start()
+    side = lax.broadcasted_iota(jnp.int32, (c, EDGE), 1)
+    for d in range(chan):
+        left, right = edges(d)
+        for r in range(2):
+            ahead, behind_it = x_ref[r, :, right].astype(F32), x_ref[r, :, left].astype(F32)
+            edge[d, r] = jnp.where(side < EDGE // 2, ahead, behind_it).astype(BF16)
     pl.semaphore_wait(barrier, chan - 1 + jnp.where(has_above, 1, 0) + jnp.where(has_below, 1, 0))
     for q in range(PIECES):
         for k in range(1, chan):
@@ -173,7 +186,8 @@
         b_copy(1, k).start()
     each_weight(0, lambda w, a, k: w_copy(w, a, k).start(), nothing)
 
-    for q in range(PIECES):
+    padded[1:3, j, :, there(0)] = edge[j]
+    for q in range(1, PIECES):
         padded[1:3, j, :, there(q)] = x_ref[:, :, across(j, q)]
     b1_all[j] = b1_ref[...]
     b2_all[j] = b2_ref[...]
@@ -187,13 +201,16 @@
     def _():
         lower[...] = jnp.zeros_like(lower)
 
-    column = lax.rem(j * part + width - EDGE, width) + lax.broadcasted_iota(jnp.int32, (1, window), 1)
+    lane = lax.broadcasted_iota(jnp.int32, (1, window), 1)
+    column = lane + jnp.where(lane < EDGE // 2, j * part + part, j * part + width - EDGE)
     column = jnp.where(column >= width, column - width, column)
     before = jnp.where(column == 0, width - 1, column - 1)
     after = jnp.where(column == width - 1, 0, column + 1)
 
     def choice(ref):
-        table = jnp.concatenate([ref[:, across(j, q)] for q in range(PIECES)], axis=1)
+        left, right = edges(j)
+        first = jnp.where(lane[:, :EDGE] < EDGE // 2, ref[:, right], ref[:, left])
+        table = jnp.concatenate([first] + [ref[:, across(j, q)] for q in range(1, PIECES)], axis=1)
         return jnp.where(table == column, 1, jnp.where(table == before, 2, jnp.where(table == after, 3, 0)))
 
     top = choice(top_ref)
@@ -241,16 +258,17 @@
     def taps(first, last):
         return wide1[:, :, :, first * channels : last * channels].reshape(3 * channels, (last - first) * channels)
 
-    def rows(first, last, at):
-        return padded[first:last, :, :, at : at + SPREAD].reshape((last - first) * channels, SPREAD)
-
-    for at in range(0, window, SPREAD):
-        inner = rows(1, 3, at)
+    def rows(first, last, here):
+        return padded[first:last, :, :, here].reshape((last - first) * channels, here.stop - here.start)
+
+    chunks = [slice(at, min(at + SPREAD, window)) for at in range(0, window, SPREAD)]
+    for here in chunks:
+        inner = rows(1, 3, here)
         for r in (1, 0):
-            totals[r, :, at : at + SPREAD] = jnp.dot(taps(1 - r, 3 - r), inner, preferred_element_type=F32)
-
-    def rim_copy():
-        return remote(hid.at[1], rim, rim_send, rim_recv, (s + 1, j))
+            totals[r, :, here] = jnp.dot(taps(1 - r, 3 - r), inner, preferred_element_type=F32)
+
+    def rim_copy(d):
+        return remote(hid.at[1, d], rim.at[d], rim_send.at[d], rim_recv.at[d], (s + 1, j))
 
     def h_copy(r, k):
         mine = pl.ds(pl.multiple_of(j * part, EDGE), part)
@@ -276,9 +294,9 @@
     for r in (1, 0):
         for k in range(1, chan):
             lower_rim(k) if r == 1 else upper_rim(k)
-        for at in range(0, window, SPREAD):
-            outer = rows(3 * r, 3 * r + 1, at)
-            totals[r, :, at : at + SPREAD] += jnp.dot(taps(2 * r, 2 * r + 1), outer, preferred_element_type=F32)
+        for here in chunks:
+            outer = rows(3 * r, 3 * r + 1, here)
+            totals[r, :, here] += jnp.dot(taps(2 * r, 2 * r + 1), outer, preferred_element_type=F32)
         for g in range(0, channels, GROUP):
             pre = (
                 pltpu.roll(totals[r, g : g + GROUP], 1, 1)
@@ -287,10 +305,10 @@
                 + bias1[g : g + GROUP]
             )
             hid[r, g // o, g % o : g % o + GROUP] = gelu(pre).astype(BF16)
-        if r == 1:
-            @pl.when(has_below)
-            def _():
-                rim_copy().start()
+            if r == 1 and (g + GROUP) % o == 0:
+                @pl.when(has_below)
+                def _():
+                    rim_copy(g // o).start()
         for k in range(1, chan):
             h_copy(r, k).start()
 
@@ -322,25 +340,36 @@
     for g in range(0, chan * o2, GROUP):
         sums[g : g + GROUP] = sums[g : g + GROUP] + shifted(g) + bias2[g : g + GROUP]
 
-    @pl.when(has_above)
-    def _():
-        rim_copy().wait_recv()
-
     for d in range(chan):
+        @pl.when(has_above)
+        def _():
+            rim_copy(d).wait_recv()
+
         remap_into(fixed.at[d], rim.at[d], top)
     split_columns(fixed[...].reshape(channels, window), 0)
     sums[...] += products(0, 1)
 
-    def p_copy(k):
+    piece = o2 // 2
+
+    def p_copy(k, h):
         mine = pl.ds(pl.multiple_of(j * half, EDGE), half)
-        return remote(result.at[peer(k)], coarse_ref.at[:, mine], p_send.at[k], p_recv.at[k], (s, peer(k)))
-
-    for g in range(0, chan * o2, GROUP):
-        result[g // o2, g % o2 : g % o2 + GROUP] = gelu(sums[g : g + GROUP] + shifted(g)).astype(BF16)
-    for k in range(1, chan):
-        p_copy(k).start()
+        these = slice(h * piece, (h + 1) * piece)
+        return remote(
+            result.at[peer(k), these], coarse_ref.at[these, mine], p_send.at[k, h], p_recv.at[k, h], (s, peer(k))
+        )
+
     ours = pl.ds(pl.multiple_of(j * half, EDGE), half)
-    coarse_ref[:, ours] = result[j]
+    for k in [*range(1, chan), 0]:
+        for h in range(2):
+            for g in range(h * piece, (h + 1) * piece, GROUP):
+                at = pl.ds(pl.multiple_of(peer(k) * o2 + g, GROUP), GROUP)
+                value = gelu(sums[at] + pltpu.roll(behind[at], 1, 1)[:, EDGE:]).astype(BF16)
+                if k == 0:
+                    coarse_ref[g : g + GROUP, ours] = value
+                else:
+                    result[peer(k), g : g + GROUP] = value
+            if k > 0:
+                p_copy(k, h).start()
 
     for k in range(1, chan):
         for q in range(PIECES):
@@ -349,7 +378,8 @@
             b_copy(which, k).wait_send()
         for r in range(2):
             h_copy(r, k).wait()
-        p_copy(k).wait()
+        for h in range(2):
+            p_copy(k, h).wait()
 
     def sent(w, a, k):
         w_copy(w, a, k).wait_send()
@@ -363,7 +393,8 @@
         for k in range(chan):
             for q in range(PIECES):
                 up_copy(k, q).wait_send()
-        rim_copy().wait_send()
+        for d in range(chan):
+            rim_copy(d).wait_send()
 
     @pl.when(has_above)
     def _():
@@ -377,7 +408,7 @@
     o, _, _, channels = first_weight.shape
     o2 = second_weight.shape[0]
     part = width // chan
-    window = part + 2 * EDGE
+    window = part + EDGE
     half = part // 2
     x = jnp.transpose(features[0], (1, 0, 2))
     w1 = jnp.transpose(first_weight, (1, 2, 0, 3))
@@ -394,6 +425,7 @@
         in_specs=[in_vmem, in_vmem, in_vmem, in_hbm, in_vmem, in_hbm, in_vmem],
         out_specs=(in_vmem, in_vmem),
         scratch_shapes=[
+            pltpu.VMEM((chan, 2, c, EDGE), BF16),
             pltpu.VMEM((4, chan, c, window), BF16),
             pltpu.VMEM((chan, c, window), BF16),
             pltpu.VMEM((chan, c, window), BF16),
@@ -418,8 +450,8 @@
             dma((chan, PIECES)),
             dma((chan, PIECES)),
             dma((chan, PIECES)),
-            dma,
-            dma,
+            dma((chan,)),
+            dma((chan,)),
             dma((2, 3)),
             dma((2, 3, chan)),
             dma((2, 3, chan)),
@@ -429,8 +461,8 @@
             dma((2, chan)),
             dma((2, chan)),
             dma((2, chan)),
-            dma((chan,)),
-            dma((chan,)),
+            dma((chan, 2)),
+            dma((chan, 2)),
         ],
         compiler_params=pltpu.CompilerParams(
             collective_id=0, has_side_effects=True, vmem_limit_bytes=40 * 1024 * 1024

time: 31.5 us -> 31.2 us (level)
  no operation moved by 1% of the time
where the time goes in v3:
time: 31.2 us; the launch traced here: 31 us
  Pallas kernels  26.4 us (85%)
  local copies, waits for them, and re-layouts  3.92 us (13%)
  between operations  0.72 us (2%)
    pallas_call x1, Pallas kernels, per_device(): pl.pallas_call(functools.partial(kernel, space, chan), out_shape=(jax.Sha...  26.4 us
    unnamed x15, local copies, waits for them, and re-layouts  3.92 us

profile of v3, /device:TPU:0, one launch (start us, length us, event | category | flops | bytes accessed | tf_op | source)
XLA Modules:
  0.0 31.0 jit_solution(13645335905562071900)
XLA Ops:
  0.6 0.0 copy-start
  0.6 0.0 copy-start.1
  0.7 0.0 copy-start.2
  0.7 0.0 copy-start.3
  0.7 1.2 %copy.12 = bf16[1,64,2,2048]{3,1,2,0:T(8,128)(2,1)S(1)} copy(bf16[1,64,2,2048]{3,2,1,0:T(2,128)(2,1)} %param.7) | data formatting | bytes 1048576 | tf_op args[0]
  1.9 0.0 copy-start.4
  1.9 0.0 copy-start.5
  1.9 0.0 copy-done
  2.0 0.0 copy-done.1
  2.0 0.0 copy-done.2
  2.0 0.0 copy-done.3
  2.0 0.6 %copy-done.4 = f32[64]{0:T(128)S(1)} copy-done((f32[64]{0:T(128)S(1)}, f32[64]{0:T(128)}, u32[]{:S(2)}) %copy-start.4) | copy-done | bytes 280
  2.6 0.0 copy-done.5
  2.6 26.4 %shard_map.86 = (bf16[2,64,2048]{2,1,0:T(8,128)(2,1)S(1)}, bf16[128,1024]{1,0:T(8,128)(2,1)S(1)}) custom-call(bf16[2,64,2048]{2,1,0:T(8,128)(2,1)S(1)} %bitcast.13, s32[1,2048]{1,0:T(1,128)S(1)} %copy-done.2, s32[1,2048]{1,0:T(1,128)S(1)} %copy-done.3, bf16[3,3,64,128]{3,2,1,0:T(8,128)(2,1)S(1)} %bitcast.17, f32[1,64]{1,0:T(1,128)S(1)} %bitcast.18, ...), custom_call_target="tpu_custom_call" | custom-call | tf_op jit(solution)/shard_map/pallas_call | solution.py:419
  29.0 1.3 %copy.10 = bf16[1,64,2,2048]{3,2,1,0:T(2,128)(2,1)} copy(bf16[1,64,2,2048]{3,1,2,0:T(8,128)(2,1)S(1)} %bitcast.14) | data formatting | bytes 1048576
  30.3 0.7 %copy.14 = bf16[1,128,1,1024]{3,1,2,0:T(8,128)(2,1)} copy(bf16[1,128,1,1024]{3,1,2,0:T(8,128)(2,1)S(1)} %bitcast.16) | data formatting | bytes 524288
Async XLA Ops:
  0.6 1.3 %copy-start = (bf16[128,3,3,128]{3,0,2,1:T(8,128)(2,1)S(1)}, bf16[128,3,3,128]{3,0,2,1:T(8,128)(2,1)}, u32[]{:S(2)}) copy-start(bf16[128,3,3,128]{3,0,2,1:T(8,128)(2,1)} %param.12) | copy-start | bytes 884740
  0.6 1.3 %copy-start.1 = (bf16[64,3,3,128]{3,0,2,1:T(8,128)(2,1)S(1)}, bf16[64,3,3,128]{3,0,2,1:T(8,128)(2,1)}, u32[]{:S(2)}) copy-start(bf16[64,3,3,128]{3,0,2,1:T(8,128)(2,1)} %param.10) | copy-start | bytes 442372
  0.7 1.3 %copy-start.2 = (s32[1,2048]{1,0:T(1,128)S(1)}, s32[1,2048]{1,0:T(1,128)}, u32[]{:S(2)}) copy-start(s32[1,2048]{1,0:T(1,128)} %top_ref.1) | copy-start | bytes 24580
  0.7 1.3 %copy-start.3 = (s32[1,2048]{1,0:T(1,128)S(1)}, s32[1,2048]{1,0:T(1,128)}, u32[]{:S(2)}) copy-start(s32[1,2048]{1,0:T(1,128)} %bottom_ref.1) | copy-start | bytes 24580
  1.9 0.7 %copy-start.4 = (f32[64]{0:T(128)S(1)}, f32[64]{0:T(128)}, u32[]{:S(2)}) copy-start(f32[64]{0:T(128)} %param.11) | copy-start | bytes 772
  1.9 0.7 %copy-start.5 = (f32[128]{0:T(128)S(1)}, f32[128]{0:T(128)}, u32[]{:S(2)}) copy-start(f32[128]{0:T(128)} %param.13) | copy-start | bytes 1540

commit v4 on v3

--- a/solution.py
+++ b/solution.py
@@ -14,6 +14,7 @@
 SPREAD = 256
 PIECES = 3
 GROUP = 16
+RIM = 4
 
 
 def gelu(v):
@@ -267,13 +268,16 @@
         for r in (1, 0):
             totals[r, :, here] = jnp.dot(taps(1 - r, 3 - r), inner, preferred_element_type=F32)
 
+    share = channels // RIM
+
     def rim_copy(d):
-        return remote(hid.at[1, d], rim.at[d], rim_send.at[d], rim_recv.at[d], (s + 1, j))
+        these = slice(d * share, (d + 1) * share)
+        return remote(hid.at[1, these], rim.at[these], rim_send.at[d], rim_recv.at[d], (s + 1, j))
 
     def h_copy(r, k):
         mine = pl.ds(pl.multiple_of(j * part, EDGE), part)
         return remote(
-            hid.at[r, peer(k), :, EDGE : EDGE + part], hidden_ref.at[r, :, mine],
+            hid.at[r, pl.ds(pl.multiple_of(peer(k) * o, GROUP), o), EDGE : EDGE + part], hidden_ref.at[r, :, mine],
             h_send.at[r, k], h_recv.at[r, k], (s, peer(k)),
         )
 
@@ -282,14 +286,15 @@
     wanted = jnp.where(wanted < SPREAD // 2, 2 * wanted, 2 * wanted - SPREAD + 1)
     picker = jnp.where(spot == wanted, 1.0, 0.0).astype(BF16)
 
-    def split_columns(row, at):
-        odd[at, :, :EDGE] = row[:, :EDGE]
+    def split_columns(row, at, begin):
+        these = slice(begin, begin + row.shape[0])
+        odd[at, these, :EDGE] = row[:, :EDGE]
         for block in range(part // SPREAD):
             first = EDGE + block * SPREAD
             both = jnp.dot(row[:, first : first + SPREAD], picker, preferred_element_type=F32).astype(BF16)
             here = block * (SPREAD // 2)
-            even[at, :, here : here + SPREAD // 2] = both[:, : SPREAD // 2]
-            odd[at, :, EDGE + here : EDGE + here + SPREAD // 2] = both[:, SPREAD // 2 :]
+            even[at, these, here : here + SPREAD // 2] = both[:, : SPREAD // 2]
+            odd[at, these, EDGE + here : EDGE + here + SPREAD // 2] = both[:, SPREAD // 2 :]
 
     for r in (1, 0):
         for k in range(1, chan):
@@ -304,18 +309,18 @@
                 + pltpu.roll(totals[r, 2 * channels + g : 2 * channels + g + GROUP], window - 1, 1)
                 + bias1[g : g + GROUP]
             )
-            hid[r, g // o, g % o : g % o + GROUP] = gelu(pre).astype(BF16)
-            if r == 1 and (g + GROUP) % o == 0:
+            hid[r, g : g + GROUP] = gelu(pre).astype(BF16)
+            if r == 1 and (g + GROUP) % share == 0:
                 @pl.when(has_below)
                 def _():
-                    rim_copy(g // o).start()
+                    rim_copy(g // share).start()
         for k in range(1, chan):
             h_copy(r, k).start()
 
     own = pl.ds(pl.multiple_of(j * part, EDGE), part)
-    hidden_ref[:, :, own] = hid[:, j, :, EDGE : EDGE + part]
-    split_columns(hid[0].reshape(channels, window), 1)
-    split_columns(hid[1].reshape(channels, window), 2)
+    hidden_ref[:, :, own] = hid[:, pl.ds(pl.multiple_of(j * o, GROUP), o), EDGE : EDGE + part]
+    split_columns(hid[0], 1, 0)
+    split_columns(hid[1], 2, 0)
     each_weight(1, arrived, nothing)
     each_weight(1, nothing, lambda w, a, k: w_pass(w, a, k).wait_recv())
     for a in range(3):
@@ -340,14 +345,13 @@
     for g in range(0, chan * o2, GROUP):
         sums[g : g + GROUP] = sums[g : g + GROUP] + shifted(g) + bias2[g : g + GROUP]
 
-    for d in range(chan):
+    for d in range(RIM):
         @pl.when(has_above)
         def _():
             rim_copy(d).wait_recv()
 
-        remap_into(fixed.at[d], rim.at[d], top)
-    split_columns(fixed[...].reshape(channels, window), 0)
-    sums[...] += products(0, 1)
+        remap_into(fixed, rim.at[d * share : (d + 1) * share], top)
+        split_columns(fixed[...], 0, d * share)
 
     piece = o2 // 2
 
@@ -360,6 +364,13 @@
 
     ours = pl.ds(pl.multiple_of(j * half, EDGE), half)
     for k in [*range(1, chan), 0]:
+        owner = peer(k)
+        block = pl.ds(pl.multiple_of(owner * o2, GROUP), o2)
+        late = wide2[:, owner, :, :channels]
+        behind[block] = jnp.dot(late[0], odd[0], preferred_element_type=F32)
+        sums[block] += jnp.dot(late[1], even[0], preferred_element_type=F32) + jnp.dot(
+            late[2], odd[0, :, EDGE:], preferred_element_type=F32
+        )
         for h in range(2):
             for g in range(h * piece, (h + 1) * piece, GROUP):
                 at = pl.ds(pl.multiple_of(peer(k) * o2 + g, GROUP), GROUP)
@@ -393,7 +404,7 @@
         for k in range(chan):
             for q in range(PIECES):
                 up_copy(k, q).wait_send()
-        for d in range(chan):
+        for d in range(RIM):
             rim_copy(d).wait_send()
 
     @pl.when(has_above)
@@ -436,9 +447,9 @@
             pltpu.VMEM((channels, 1), F32),
             pltpu.VMEM((chan * o2, 1), F32),
             pltpu.VMEM((2, 3 * channels, window), F32),
-            pltpu.VMEM((2, chan, o, window), BF16),
-            pltpu.VMEM((chan, o, window), BF16),
-            pltpu.VMEM((chan, o, window), BF16),
+            pltpu.VMEM((2, channels, window), BF16),
+            pltpu.VMEM((channels, window), BF16),
+            pltpu.VMEM((channels // RIM, window), BF16),
             pltpu.VMEM((3, channels, half), BF16),
             pltpu.VMEM((3, channels, EDGE + half), BF16),
             pltpu.VMEM((chan * o2, half), F32),
@@ -450,8 +461,8 @@
             dma((chan, PIECES)),
             dma((chan, PIECES)),
             dma((chan, PIECES)),
-            dma((chan,)),
-            dma((chan,)),
+            dma((RIM,)),
+            dma((RIM,)),
             dma((2, 3)),
             dma((2, 3, chan)),
             dma((2, 3, chan)),

time: 31.2 us -> 31.8 us (1.019)
  Pallas kernels: 26.4 us -> 27 us
    pallas_call x1, Pallas kernels: 26.4 us -> 27 us  [per_device(): pl.pallas_call(functools.partial(kernel, space, chan), out_shape=(jax.Sha...]
where the time goes in v4:
time: 31.8 us; the launch traced here: 31.6 us
  Pallas kernels  27 us (85%)
  local copies, waits for them, and re-layouts  3.92 us (12%)
  between operations  0.72 us (2%)
    pallas_call x1, Pallas kernels, per_device(): pl.pallas_call(functools.partial(kernel, space, chan), out_shape=(jax.Sha...  27 us
    unnamed x15, local copies, waits for them, and re-layouts  3.92 us

profile of v4, /device:TPU:0, one launch (start us, length us, event | category | flops | bytes accessed | tf_op | source)
XLA Modules:
  0.0 31.6 jit_solution(1370744453165638843)
XLA Ops:
  0.6 0.0 copy-start
  0.6 0.0 copy-start.1
  0.7 0.0 copy-start.2
  0.7 0.0 copy-start.3
  0.7 1.2 %copy.12 = bf16[1,64,2,2048]{3,1,2,0:T(8,128)(2,1)S(1)} copy(bf16[1,64,2,2048]{3,2,1,0:T(2,128)(2,1)} %param.7) | data formatting | bytes 1048576 | tf_op args[0]
  1.9 0.0 copy-start.4
  1.9 0.0 copy-start.5
  1.9 0.0 copy-done
  2.0 0.0 copy-done.1
  2.0 0.0 copy-done.2
  2.0 0.0 copy-done.3
  2.0 0.6 %copy-done.4 = f32[64]{0:T(128)S(1)} copy-done((f32[64]{0:T(128)S(1)}, f32[64]{0:T(128)}, u32[]{:S(2)}) %copy-start.4) | copy-done | bytes 280
  2.6 0.0 copy-done.5
  2.6 27.0 %shard_map.86 = (bf16[2,64,2048]{2,1,0:T(8,128)(2,1)S(1)}, bf16[128,1024]{1,0:T(8,128)(2,1)S(1)}) custom-call(bf16[2,64,2048]{2,1,0:T(8,128)(2,1)S(1)} %bitcast.13, s32[1,2048]{1,0:T(1,128)S(1)} %copy-done.2, s32[1,2048]{1,0:T(1,128)S(1)} %copy-done.3, bf16[3,3,64,128]{3,2,1,0:T(8,128)(2,1)S(1)} %bitcast.17, f32[1,64]{1,0:T(1,128)S(1)} %bitcast.18, ...), custom_call_target="tpu_custom_call" | custom-call | tf_op jit(solution)/shard_map/pallas_call | solution.py:430
  29.6 1.3 %copy.10 = bf16[1,64,2,2048]{3,2,1,0:T(2,128)(2,1)} copy(bf16[1,64,2,2048]{3,1,2,0:T(8,128)(2,1)S(1)} %bitcast.14) | data formatting | bytes 1048576
  30.9 0.7 %copy.14 = bf16[1,128,1,1024]{3,1,2,0:T(8,128)(2,1)} copy(bf16[1,128,1,1024]{3,1,2,0:T(8,128)(2,1)S(1)} %bitcast.16) | data formatting | bytes 524288
Async XLA Ops:
  0.6 1.3 %copy-start = (bf16[128,3,3,128]{3,0,2,1:T(8,128)(2,1)S(1)}, bf16[128,3,3,128]{3,0,2,1:T(8,128)(2,1)}, u32[]{:S(2)}) copy-start(bf16[128,3,3,128]{3,0,2,1:T(8,128)(2,1)} %param.12) | copy-start | bytes 884740
  0.6 1.3 %copy-start.1 = (bf16[64,3,3,128]{3,0,2,1:T(8,128)(2,1)S(1)}, bf16[64,3,3,128]{3,0,2,1:T(8,128)(2,1)}, u32[]{:S(2)}) copy-start(bf16[64,3,3,128]{3,0,2,1:T(8,128)(2,1)} %param.10) | copy-start | bytes 442372
  0.7 1.3 %copy-start.2 = (s32[1,2048]{1,0:T(1,128)S(1)}, s32[1,2048]{1,0:T(1,128)}, u32[]{:S(2)}) copy-start(s32[1,2048]{1,0:T(1,128)} %top_ref.1) | copy-start | bytes 24580
  0.7 1.3 %copy-start.3 = (s32[1,2048]{1,0:T(1,128)S(1)}, s32[1,2048]{1,0:T(1,128)}, u32[]{:S(2)}) copy-start(s32[1,2048]{1,0:T(1,128)} %bottom_ref.1) | copy-start | bytes 24580
  1.9 0.7 %copy-start.4 = (f32[64]{0:T(128)S(1)}, f32[64]{0:T(128)}, u32[]{:S(2)}) copy-start(f32[64]{0:T(128)} %param.11) | copy-start | bytes 772
  1.9 0.7 %copy-start.5 = (f32[128]{0:T(128)S(1)}, f32[128]{0:T(128)}, u32[]{:S(2)}) copy-start(f32[128]{0:T(128)} %param.13) | copy-start | bytes 1540

commit v5 on v3

--- a/solution.py
+++ b/solution.py
@@ -116,13 +116,13 @@
         return remote(src, lower.at[source(k), :, there(q)], low_send.at[k, q], low_recv.at[k, q], (s - 1, j))
 
     def pass_on(k, q):
+        @pl.when(has_above)
+        def _():
+            low_copy(k, q).start()
+
         @pl.when(has_below)
         def _():
             up_copy(k, q).start()
-
-        @pl.when(has_above)
-        def _():
-            low_copy(k, q).start()
 
     def place(which, owner, a):
         wide = (wide1, wide2)[which]
@@ -177,6 +177,8 @@
             edge[d, r] = jnp.where(side < EDGE // 2, ahead, behind_it).astype(BF16)
     pl.semaphore_wait(barrier, chan - 1 + jnp.where(has_above, 1, 0) + jnp.where(has_below, 1, 0))
     for q in range(PIECES):
+        if q == PIECES - 1:
+            each_weight(0, lambda w, a, k: w_copy(w, a, k).start(), nothing)
         for k in range(1, chan):
             x_copy(k, q).start()
     for q in range(PIECES):
@@ -184,7 +186,6 @@
     for k in range(1, chan):
         b_copy(0, k).start()
         b_copy(1, k).start()
-    each_weight(0, lambda w, a, k: w_copy(w, a, k).start(), nothing)
 
     padded[1:3, j, :, there(0)] = edge[j]
     for q in range(1, PIECES):
@@ -234,17 +235,17 @@
 
     lower_rim(0)
     upper_rim(0)
+    def arrived(w, a, k):
+        w_copy(w, a, k).wait_recv()
+        w_pass(w, a, k).start()
+
     for q in range(PIECES):
+        if q == PIECES - 1:
+            each_weight(0, arrived, nothing)
         for k in range(1, chan):
             x_copy(k, q).wait_recv()
             pass_on(k, q)
     each_weight(1, lambda w, a, k: w_copy(w, a, k).start(), nothing)
-
-    def arrived(w, a, k):
-        w_copy(w, a, k).wait_recv()
-        w_pass(w, a, k).start()
-
-    each_weight(0, arrived, nothing)
     each_weight(0, nothing, lambda w, a, k: w_pass(w, a, k).wait_recv())
     for a in range(3):
         w_own(0, a).wait()

time: 31.2 us -> 31.7 us (1.016)
    pallas_call x1, Pallas kernels: 26.4 us -> 26.7 us  [per_device(): pl.pallas_call(functools.partial(kernel, space, chan), out_shape=(jax.Sha...]
where the time goes in v5:
time: 31.7 us; the launch traced here: 31.4 us
  Pallas kernels  26.7 us (84%)
  local copies, waits for them, and re-layouts  3.92 us (12%)
  between operations  0.72 us (2%)
    pallas_call x1, Pallas kernels, per_device(): pl.pallas_call(functools.partial(kernel, space, chan), out_shape=(jax.Sha...  26.7 us
    unnamed x15, local copies, waits for them, and re-layouts  3.92 us

profile of v5, /device:TPU:0, one launch (start us, length us, event | category | flops | bytes accessed | tf_op | source)
XLA Modules:
  0.0 31.4 jit_solution(12771873857846060303)
XLA Ops:
  0.6 0.0 copy-start
  0.6 0.0 copy-start.1
  0.7 0.0 copy-start.2
  0.7 0.0 copy-start.3
  0.7 1.2 %copy.12 = bf16[1,64,2,2048]{3,1,2,0:T(8,128)(2,1)S(1)} copy(bf16[1,64,2,2048]{3,2,1,0:T(2,128)(2,1)} %param.7) | data formatting | bytes 1048576 | tf_op args[0]
  1.9 0.0 copy-start.4
  1.9 0.0 copy-start.5
  1.9 0.0 copy-done
  2.0 0.0 copy-done.1
  2.0 0.0 copy-done.2
  2.0 0.0 copy-done.3
  2.0 0.6 %copy-done.4 = f32[64]{0:T(128)S(1)} copy-done((f32[64]{0:T(128)S(1)}, f32[64]{0:T(128)}, u32[]{:S(2)}) %copy-start.4) | copy-done | bytes 280
  2.6 0.0 copy-done.5
  2.6 26.7 %shard_map.86 = (bf16[2,64,2048]{2,1,0:T(8,128)(2,1)S(1)}, bf16[128,1024]{1,0:T(8,128)(2,1)S(1)}) custom-call(bf16[2,64,2048]{2,1,0:T(8,128)(2,1)S(1)} %bitcast.13, s32[1,2048]{1,0:T(1,128)S(1)} %copy-done.2, s32[1,2048]{1,0:T(1,128)S(1)} %copy-done.3, bf16[3,3,64,128]{3,2,1,0:T(8,128)(2,1)S(1)} %bitcast.17, f32[1,64]{1,0:T(1,128)S(1)} %bitcast.18, ...), custom_call_target="tpu_custom_call" | custom-call | tf_op jit(solution)/shard_map/pallas_call | solution.py:420
  29.3 1.3 %copy.10 = bf16[1,64,2,2048]{3,2,1,0:T(2,128)(2,1)} copy(bf16[1,64,2,2048]{3,1,2,0:T(8,128)(2,1)S(1)} %bitcast.14) | data formatting | bytes 1048576
  30.7 0.7 %copy.14 = bf16[1,128,1,1024]{3,1,2,0:T(8,128)(2,1)} copy(bf16[1,128,1,1024]{3,1,2,0:T(8,128)(2,1)S(1)} %bitcast.16) | data formatting | bytes 524288
Async XLA Ops:
  0.6 1.3 %copy-start = (bf16[128,3,3,128]{3,0,2,1:T(8,128)(2,1)S(1)}, bf16[128,3,3,128]{3,0,2,1:T(8,128)(2,1)}, u32[]{:S(2)}) copy-start(bf16[128,3,3,128]{3,0,2,1:T(8,128)(2,1)} %param.12) | copy-start | bytes 884740
  0.6 1.3 %copy-start.1 = (bf16[64,3,3,128]{3,0,2,1:T(8,128)(2,1)S(1)}, bf16[64,3,3,128]{3,0,2,1:T(8,128)(2,1)}, u32[]{:S(2)}) copy-start(bf16[64,3,3,128]{3,0,2,1:T(8,128)(2,1)} %param.10) | copy-start | bytes 442372
  0.7 1.3 %copy-start.2 = (s32[1,2048]{1,0:T(1,128)S(1)}, s32[1,2048]{1,0:T(1,128)}, u32[]{:S(2)}) copy-start(s32[1,2048]{1,0:T(1,128)} %top_ref.1) | copy-start | bytes 24580
  0.7 1.3 %copy-start.3 = (s32[1,2048]{1,0:T(1,128)S(1)}, s32[1,2048]{1,0:T(1,128)}, u32[]{:S(2)}) copy-start(s32[1,2048]{1,0:T(1,128)} %bottom_ref.1) | copy-start | bytes 24580
  1.9 0.7 %copy-start.4 = (f32[64]{0:T(128)S(1)}, f32[64]{0:T(128)}, u32[]{:S(2)}) copy-start(f32[64]{0:T(128)} %param.11) | copy-start | bytes 772
  1.9 0.7 %copy-start.5 = (f32[128]{0:T(128)S(1)}, f32[128]{0:T(128)}, u32[]{:S(2)}) copy-start(f32[128]{0:T(128)} %param.13) | copy-start | bytes 1540
